TPU v7x, 32 devices: a whole 2x2x4 slice. The times are simulated.
32 devices in a mesh: row: 8 (over y, x, core), help: 4 (over z).
Axes of the slice: x: 2, y: 2, z: 4, core: 2. Of those that a mesh axis runs over, the one named last changes fastest.
Arguments:
- points: float32 [32, 4, 1024], P(('row', 'help')), as said below
- sketch: bfloat16 [8, 4, 8, 2, 1024, 256], P('row', 'help'), may hold values from -6 to 6
- slots: int32 [8, 4, 8, 2], P('row', 'help'), may hold values from -1 to 3, as said below
- ranks: int32 [32], P(('row', 'help')), may hold values from 32 to 256
Outputs:
- block_row_sketches: float32 [32, 1024, 256], P(('row', 'help'))
- gram: float32 [32, 256, 256], P(('row', 'help'))
Inputs may be any that keep to these rules, and one draw needn't show every extreme that they name: For c = group * 4 + column, each of points[c, 0:3] lies within 1.5 of the matching coordinate of (column / 4, (group % 4) / 4, (group // 4) / 4); points[c, 3] lie in [0.05, 1]. `slots`: a named column differs from the source's column c; the 2 entries [g, c, r, :] that are named differ; for some c and r all 16 entries [:, c, r, :] are named.
All inputs are finite; a program needn't handle non-finite values.
Results may differ from a plain program's by a relative error of at most 0.0029.
Values may be sent and summed in bfloat16 or wider, within the bound.
A program may use at most 128 MiB of HBM per device.

v0:
```python
import jax
import jax.numpy as jnp
from jax import lax
from jax.sharding import PartitionSpec as P

decay_rate = 0.3
four_pi = 12.566370614359172
soften = 0.0025
batch_slots = 8


def kernel_tile(target, source):
    offset_along_x = target[0][:, None] - source[0][None, :]
    delta_y = target[1][:, None] - source[1][None, :]
    offset_along_z = target[2][:, None] - source[2][None, :]
    distance = jnp.sqrt(
        offset_along_x * offset_along_x
        + delta_y * delta_y
        + offset_along_z * offset_along_z
        + soften
    )
    values = jnp.exp(-decay_rate * distance) / (four_pi * distance) * source[3][None, :]
    return values.astype(jnp.bfloat16)


def multiply(tiles, blocks):
    return jnp.einsum("bpq,bqw->bpw", tiles, blocks, preferred_element_type=jnp.float32)


def slot_order(labels, size):
    total = labels.shape[0]
    blocks_count = -(-total // size)
    padded = blocks_count * size
    order = jnp.argsort((labels < 0).astype(jnp.int32), stable=True)
    live_count = jnp.sum((labels >= 0).astype(jnp.int32))
    turns = (live_count + size - 1) // size
    order = jnp.concatenate([order, jnp.zeros((padded - total,), jnp.int32)])
    valid = jnp.arange(padded, dtype=jnp.int32) < total
    chosen_labels = jnp.where(valid, labels[order], -1).astype(jnp.int32)
    return (order.reshape(blocks_count, size), chosen_labels.reshape(blocks_count, size), turns)


def one_hot(labels, helpers):
    return (labels[:, None] == jnp.arange(helpers, dtype=jnp.int32)[None, :]).astype(jnp.float32)


def per_device(points, sketch, slots, ranks):
    panels = points.shape[2]
    width = sketch.shape[5]
    groups = sketch.shape[2]
    count = sketch.shape[3]
    helpers = lax.axis_size("help")
    total = groups * count
    size = min(batch_slots, total)
    tile_many = jax.vmap(kernel_tile)
    empty = jnp.zeros((helpers, panels, width), jnp.float32)
    targets, target_ranks = (
        lax.all_gather(points, "help", axis=0, tiled=True),
        lax.all_gather(ranks, "help", axis=0, tiled=True),
    )
    source_points = lax.all_gather(points, "row", axis=0, tiled=True)
    arrived, labels = (
        lax.all_to_all(sketch, "row", split_axis=2, concat_axis=0, tiled=True),
        lax.all_to_all(slots, "row", split_axis=2, concat_axis=0, tiled=True),
    )
    arrived = arrived.reshape(total, panels, width)
    labels = labels.reshape(total)
    order, block_labels, turns = slot_order(labels, size)

    def step(turn, sums):
        indices = order[turn]
        batch_labels = block_labels[turn]
        chosen = jnp.maximum(batch_labels, 0)
        tiles = tile_many(targets[chosen], source_points[indices // count])
        products = multiply(tiles, arrived[indices])
        return sums + jnp.einsum(
            "bh,bpw->hpw", one_hot(batch_labels, helpers), products, precision=lax.Precision.HIGHEST
        )

    sums = lax.fori_loop(0, turns, step, empty)
    mine = lax.psum_scatter(sums, "help", scatter_dimension=0, tiled=True)
    keep = jnp.arange(width, dtype=jnp.int32)[None, None, :] < ranks[:, None, None]
    block_row_sketches = jnp.where(keep, mine, jnp.zeros_like(mine))
    gram = jnp.einsum(
        "usv,usw->uvw", block_row_sketches, block_row_sketches, precision=lax.Precision.HIGHEST
    )
    return (block_row_sketches, gram)


def solution(mesh):
    in_specs = (
        P(("row", "help"), None, None),
        P("row", "help", None, None, None, None),
        P("row", "help", None, None),
        P(("row", "help")),
    )
    out_specs = (P(("row", "help"), None, None), P(("row", "help"), None, None))
    return jax.shard_map(
        per_device, mesh=mesh, in_specs=in_specs, out_specs=out_specs, check_vma=False
    )
```

profile of v0, /device:TPU:0, one launch (start us, length us, event | category | flops | bytes accessed | tf_op | source)
XLA Modules:
  0.0 322.7 jit_solution(6638196532238847147)
XLA Ops:
  7.2 0.8 copy.11
  7.9 9.6 %all_to_all.8 = s32[1,1,8,2]{3,1,0,2:T(1,128)S(1)} all-to-all(s32[1,1,8,2]{3,1,0,2:T(1,128)S(1)} %copy.11), channel_id=1, replica_groups=mesh['row'=8,'help'=4] {'row'}, dimensions={2} | all-to-all | bytes 128 | tf_op jit(solution)/shard_map/all_to_all | solution.py:64
  17.5 0.0 copy-start.1
  17.5 5.1 %all-to-all-start.1 = ((bf16[1,1,8,2,1024,256]{5,4,3,1,0,2:T(8,128)(2,1)}), bf16[1,1,8,2,1024,256]{5,4,3,1,0,2:T(8,128)(2,1)}, u32[]{:S(2)}, u32[]{:S(2)}) async-start(bf16[1,1,8,2,1024,256]{5,4,3,1,0,2:T(8,128)(2,1)} %bitcast.74), calls=%async_computation.1 | async-start | bytes 16777216 | tf_op jit(solution)/shard_map/all_to_all | solution.py:63
  22.6 0.0 reduce-scatter.2.cloned.1.call-start
  22.7 0.0 copy-done.1
  22.7 13.4 %all_gather.6 = f32[4,4,1024]{2,1,0:T(4,128)S(1)} all-gather(f32[1,4,1024]{2,1,0:T(4,128)S(1)} %copy-done.1), channel_id=1, replica_groups=mesh['row'=8,'help'=4] {'help'}, dimensions={0}, use_global_device_ids=true | all-gather | bytes 81920 | tf_op jit(solution)/shard_map/all_gather | solution.py:58
  36.1 84.0 %all_gather.7 = f32[8,4,1024]{2,1,0:T(4,128)S(1)} all-gather(f32[1,4,1024]{2,1,0:T(4,128)S(1)} %copy-done.1), channel_id=1, replica_groups=mesh['row'=8,'help'=4] {'row'}, dimensions={0}, use_global_device_ids=true | all-gather | bytes 147456 | tf_op jit(solution)/shard_map/all_gather | solution.py:61
  120.0 0.5 broadcast.222
  120.6 1.3 fusion.27
  122.5 0.1 reshape.175
  122.6 1.2 sort.17
  123.8 0.1 reshape.176
  123.9 0.7 gather_fusion.3
  124.6 0.1 gather.24
  124.7 0.0 all-to-all-done.1
  124.7 2.5 broadcast_in_dim.28
  127.2 51.3 %while.12 = (s32[]{:T(128)}, f32[4,1024,256]{2,0,1:T(4,128)}, s32[]{:T(128)}, s32[2,8]{1,0:T(2,128)S(1)}, f32[4,4,1024]{2,1,0:T(4,128)S(1)}, /*index=5*/s32[2,8]...) while((s32[]{:T(128)}, f32[4,1024,256]{2,0,1:T(4,128)}, ...), condition=%wide.region_3.4_spmd, body=%wide.region_2.3_spmd.sunk | while | flops 4514122752 | bytes 39432760 | solution.py:80
  127.2 0.6 gather_fusion.2
  127.9 0.1 fusion.46
  128.0 0.6 gather_fusion.1
  128.6 0.1 fusion.44
  128.8 6.2 %gather_fusion = bf16[8,1024,256]{2,1,0:T(8,128)(2,1)} fusion(bf16[16,1024,256]{2,1,0:T(8,128)(2,1)} %get-tuple-element.252, s32[1024]{0:T(1024)S(1)} %get-tuple-element.210), kind=kCustom, calls=%fused_computation.2.clone.1 | custom fusion | bytes 8388640 | tf_op jit(solution)/shard_map/while/body/gather | solution.py:75
  135.0 32.9 %fusion.47 = f32[8,1024,256]{2,1,0:T(8,128)S(1)} fusion(bf16[8,1024,256]{2,1,0:T(8,128)(2,1)} %gather_fusion, f32[8,1024]{1,0:T(8,128)S(1)} %bitcast.75, f32[8,1024]{1,0:T(8,128)S(1)} %bitcast.76, f32[8,1024]{1,0:T(8,128)S(1)} %get-tuple-element.217, f32[8,1024]{1,0:T(8,128)S(1)} %bitcast.77, f32[8,1024]{1,0:T(8,128)S(1)} %get-tuple-element.219, ...), kind=kOutput, calls=%fused_computation.5.clone.1 | convolution fusion | flops 4412407808 | bytes 12812288 | tf_op jit(solution)/shard_map/while/body/bpq,bqw->bpw/dot_general | solution.py:27
  167.9 10.6 %fusion.48 = f32[4,1024,256]{2,0,1:T(4,128)} fusion(f32[4,1024,256]{2,0,1:T(4,128)} %get-tuple-element.235, f32[8,1024,256]{2,1,0:T(8,128)S(1)} %fusion.47, s32[8]{0:T(128)S(1)} %get-tuple-element.222), kind=kOutput, calls=%fused_computation.18.clone.1 | convolution fusion | flops 101711904 | bytes 16777248 | tf_op jit(solution)/shard_map/while/body/bh,bpw->hpw/dot_general | solution.py:76
  178.5 4.9 %copy.13 = f32[4,1024,256]{2,1,0:T(8,128)} copy(f32[4,1024,256]{2,0,1:T(4,128)} %get-tuple-element.109) | data formatting | bytes 8388608 | tf_op jit(solution)/shard_map/while | solution.py:80
  183.5 0.0 reduce-scatter.2.cloned.1.call-update
  184.2 127.9 %reduce-scatter.2.cloned.1.call-done = f32[1,1024,256]{2,1,0:T(8,128)} async-done(((f32[4,1024,256]{2,1,0:T(8,128)}), f32[1,1024,256]{2,1,0:T(8,128)}) %reduce-scatter.2.cloned.1.call-update) | async-done | bytes 1048592 | tf_op jit(solution)/shard_map/reduce_scatter | solution.py:81
  312.0 1.3 broadcast_select_fusion
  313.3 0.0 copy-start
  313.3 2.5 convolution_bitcast_fusion
  315.9 0.0 copy-done
  (16 shorter events, 0.1 us)
Async XLA Ops:
  17.5 5.2 %copy-start.1 = (f32[1,4,1024]{2,1,0:T(4,128)S(1)}, f32[1,4,1024]{2,1,0:T(4,128)}, u32[]{:S(2)}) copy-start(f32[1,4,1024]{2,1,0:T(4,128)} %param.6) | copy-start | bytes 49156
  17.5 107.2 %all-to-all-start.1 = ((bf16[1,1,8,2,1024,256]{5,4,3,1,0,2:T(8,128)(2,1)}), bf16[1,1,8,2,1024,256]{5,4,3,1,0,2:T(8,128)(2,1)}, u32[]{:S(2)}, u32[]{:S(2)}) async-start(bf16[1,1,8,2,1024,256]{5,4,3,1,0,2:T(8,128)(2,1)} %bitcast.74), calls=%async_computation.1 | async-start | bytes 16777216 | tf_op jit(solution)/shard_map/all_to_all | solution.py:63
  22.6 289.4 %reduce-scatter.2.cloned.1.call-start = ((), (), s32[]{:S(2)}) async-start(), calls=%async_computation.3 | async-start | bytes 5242880 | tf_op jit(solution)/shard_map/reduce_scatter | solution.py:81
  313.3 2.6 copy-start
Sparse Core Ops, SparseCore 0:
  183.6 128.3 reduce-scatter.1
where the time goes:
time: 323 us
  waiting for transfers between devices  128 us (40%)
  blocking collectives  107 us (33%)
  matrix products  46.1 us (14%)
  local copies, waits for them, and re-layouts  17.2 us (5%)
  between operations  15.4 us (5%)
  starting transfers between devices  5.14 us (2%)
  other arithmetic  3.9 us (1%)
    reduce_scatter x1, waiting for transfers between devices, per_device(): mine = lax.psum_scatter(sums, 'help', scatter_dimension=0, tiled=True)  128 us
    all_gather x1, blocking collectives, per_device(): source_points = lax.all_gather(points, 'row', axis=0, tiled=True)  84 us
    dot_general x1, matrix products, multiply(): jnp.einsum('bpq,bqw->bpw', tiles, blocks, preferred_element_type=jnp.floa...  32.9 us
    all_gather x1, blocking collectives, per_device(): lax.all_gather(points, 'help', axis=0, tiled=True)  13.4 us
    dot_general x1, matrix products, step(): jnp.einsum('bh,bpw->hpw', one_hot(batch_labels, helpers), products, preci...  10.6 us
    all_to_all x1, blocking collectives, per_device(): lax.all_to_all(slots, 'row', split_axis=2, concat_axis=0, tiled=True)  9.62 us
  transfers between devices with their start and end apart: 2, of which 1 were waited for; matrix products, arithmetic and copies ran while one was open for 1% of the time, Pallas kernels for 0%

commit v1 on v0

v1 whole, which is shorter than its diff:
```python
import functools

import jax
import jax.numpy as jnp
from jax import lax
from jax.experimental import pallas as pl
from jax.experimental.pallas import tpu as pltpu
from jax.sharding import PartitionSpec as P

decay_rate = 0.3
four_pi = 12.566370614359172
soften = 0.0025
log2_e = 1.4426950408889634
centre = 0.4
MESH = pl.DeviceIdType.MESH


def cut(value):
    first = lax.reduce_precision(value, 8, 7)
    rest = value - first
    second = lax.reduce_precision(rest, 8, 7)
    third = lax.reduce_precision(rest - second, 8, 7)
    return first, second, third


def kernel(
    sizes,
    sketch_ref, spots_ref, feats_ref, logw_ref, hot_ref,
    sums_ref,
    sk_own, sk_got, spots, feats_got, logw_got, hot_got,
    lhs, acc, q_send, q_recv, q_own, z_send, z_recv,
    own_sem, sk_send_sem, sk_recv_sem, spot_send_sem, spot_recv_sem,
    side_send_sem, side_recv_sem, q_send_sem, q_recv_sem, z_send_sem, z_recv_sem,
):
    chips, helpers, slots, chunk, chunks, width = sizes
    others = helpers - 1
    row = lax.axis_index("row")
    col = lax.axis_index("help")
    chip, core = row // 2, row % 2
    sibling = chip * 2 + 1 - core
    peers = chips * helpers

    def place(step):
        return (lax.rem(chip + step // helpers, chips), lax.rem(col + step % helpers, helpers))

    def back(step):
        return (
            lax.rem(chip + chips - step // helpers, chips),
            lax.rem(col + helpers - step % helpers, helpers),
        )

    barrier = pltpu.get_barrier_semaphore()

    @pl.loop(1, peers)
    def _(step):
        to_chip, to_col = place(step)
        pl.semaphore_signal(barrier, inc=1, device_id=(to_chip * 2 + core, to_col), device_id_type=MESH)

    pl.semaphore_signal(barrier, inc=1, device_id=(sibling, col), device_id_type=MESH)
    pl.semaphore_wait(barrier, peers)

    def spot_copy(step):
        to_chip, to_col = place(step)
        return pltpu.make_async_remote_copy(
            src_ref=spots_ref,
            dst_ref=spots.at[chip * helpers + col],
            send_sem=spot_send_sem.at[step],
            recv_sem=spot_recv_sem.at[step],
            device_id=(to_chip * 2 + core, to_col),
            device_id_type=MESH,
        )

    def spot_arrival(step):
        from_chip, from_col = back(step)
        return pltpu.make_async_remote_copy(
            src_ref=spots_ref,
            dst_ref=spots.at[from_chip * helpers + from_col],
            send_sem=spot_send_sem.at[step],
            recv_sem=spot_recv_sem.at[step],
            device_id=(from_chip * 2 + core, from_col),
            device_id_type=MESH,
        )

    def to_sibling(source, target, index):
        return pltpu.make_async_remote_copy(
            src_ref=source,
            dst_ref=target,
            send_sem=side_send_sem.at[index],
            recv_sem=side_recv_sem.at[index],
            device_id=(sibling, col),
            device_id_type=MESH,
        )

    sides = (
        to_sibling(feats_ref, feats_got, 0),
        to_sibling(logw_ref, logw_got, 1),
        to_sibling(hot_ref.at[:, 1 - core], hot_got, 2),
    )

    def sketch_copy(offset):
        group = lax.rem(chip + offset, chips)
        return pltpu.make_async_remote_copy(
            src_ref=sketch_ref.at[group, 1 - core],
            dst_ref=sk_got.at[group],
            send_sem=sk_send_sem.at[offset],
            recv_sem=sk_recv_sem.at[offset],
            device_id=(sibling, col),
            device_id_type=MESH,
        )

    def own_copy(offset):
        group = lax.rem(chip + offset, chips)
        return pltpu.make_async_copy(sketch_ref.at[group, core], sk_own.at[group], own_sem.at[offset])

    own_spot = pltpu.make_async_copy(spots_ref, spots.at[chip * helpers + col], own_sem.at[chips])
    own_spot.start()

    @pl.loop(1, peers)
    def _(step):
        spot_copy(step).start()

    for side in sides:
        side.start()

    @pl.loop(0, chips)
    def _(turn):
        offset = chips - 1 - turn
        sketch_copy(offset).start()
        own_copy(offset).start()

    lhs[...] = jnp.where(
        lax.broadcasted_iota(jnp.int32, lhs.shape, 1) == 4, jnp.float32(1), jnp.float32(0)
    )
    own_spot.wait()
    for side in sides:
        side.wait()

    @pl.loop(1, peers)
    def _(step):
        spot_copy(step).wait_send()
        spot_arrival(step).wait_recv()

    def q_copy(index, offset):
        to_chip = lax.rem(chip + offset, chips)
        return pltpu.make_async_remote_copy(
            src_ref=q_send.at[index % 2, offset - 1],
            dst_ref=q_recv.at[index, offset - 1],
            send_sem=q_send_sem.at[index % 2, offset - 1],
            recv_sem=q_recv_sem.at[index, offset - 1],
            device_id=(to_chip * 2 + core, col),
            device_id_type=MESH,
        )

    def z_copy(index, step):
        return pltpu.make_async_remote_copy(
            src_ref=z_send.at[index, step],
            dst_ref=z_recv.at[index, step],
            send_sem=z_send_sem.at[index, step],
            recv_sem=z_recv_sem.at[index, step],
            device_id=(row, lax.rem(col + 1 + step, helpers)),
            device_id_type=MESH,
        )

    def block(index, group, sketches, feats, logw, hot_rows, slot, first):
        rows = pl.ds(pl.multiple_of(index * chunk, chunk), chunk)
        spot = jnp.zeros((4, chunk), jnp.float32)
        hots = []
        for step in range(others):
            hot = hot_rows(slot * others + step)
            hots.append(hot)
            target = group * helpers + lax.rem(col + 1 + step, helpers)
            spot = spot + hot[:, :chunk] * spots[target, :, rows]
        lhs[slot if first else slots + slot, 0:4, :] = spot
        full = lhs[slot if first else slots + slot]
        one = full.astype(jnp.bfloat16).astype(jnp.float32)
        rest = full - one
        two = rest.astype(jnp.bfloat16).astype(jnp.float32)
        three = rest - two
        stack = jnp.concatenate([one, one, two, two, one, three], axis=0)
        left = stack.T.astype(jnp.bfloat16)
        square = jnp.dot(left, feats, preferred_element_type=jnp.float32)
        inverse = lax.rsqrt(square)
        tile = (jnp.exp2(logw - square * inverse) * inverse).astype(jnp.bfloat16)
        product = jnp.dot(tile, sketches, preferred_element_type=jnp.float32)
        return [hot[:, :width] * product for hot in hots]

    def compute(index, offset):
        group = lax.rem(chip + offset, chips)
        totals = [None] * others
        for slot in range(slots):
            for first in (True, False):
                if first:
                    parts = block(
                        index, group, sk_own[group, slot], feats_ref[...], logw_ref[...],
                        lambda place: hot_ref[group, core, place], slot, True,
                    )
                else:
                    parts = block(
                        index, group, sk_got[group, slot], feats_got[...], logw_got[...],
                        lambda place: hot_got[group, place], slot, False,
                    )
                for step in range(others):
                    totals[step] = parts[step] if totals[step] is None else totals[step] + parts[step]
        for step in range(others):
            acc[step] = totals[step]

    def gather(index):
        @pl.loop(1, chips)
        def _(offset):
            q_copy(index, offset).wait_recv()

        for step in range(others):
            def add(offset, total):
                return total + q_recv[index, offset, step].astype(jnp.float32)

            total = lax.fori_loop(0, chips - 1, add, q_own[index % 2, step])
            z_send[index, step] = total.astype(jnp.bfloat16)
            z_copy(index, step).start()

    def finish(index):
        total = None
        for step in range(others):
            z_copy(index, step).wait_recv()
            part = z_recv[index, step].astype(jnp.float32)
            total = part if total is None else total + part
        rows = pl.ds(pl.multiple_of(index * chunk, chunk), chunk)
        sums_ref[rows, :] = total

    @pl.loop(0, chunks)
    def _(index):
        @pl.loop(0, chips)
        def _(turn):
            offset = chips - 1 - turn

            @pl.when(index == 0)
            def _():
                own_copy(offset).wait()
                sketch_copy(offset).wait()

            compute(index, offset)

            @pl.when(offset > 0)
            def _():
                @pl.when(index >= 2)
                def _():
                    q_copy(index, offset).wait_send()

                for step in range(others):
                    q_send[index % 2, offset - 1, step] = acc[step].astype(jnp.bfloat16)
                q_copy(index, offset).start()

            @pl.when(offset == 0)
            def _():
                for step in range(others):
                    q_own[index % 2, step] = acc[step]

        @pl.when(index >= 1)
        def _():
            gather(index - 1)

        @pl.when(index >= 2)
        def _():
            finish(index - 2)

    gather(chunks - 1)
    finish(chunks - 2)
    finish(chunks - 1)

    for index in (chunks - 2, chunks - 1):
        @pl.loop(1, chips)
        def _(offset):
            q_copy(index, offset).wait_send()

    @pl.loop(0, chunks)
    def _(index):
        for step in range(others):
            z_copy(index, step).wait_send()


def per_device(points, sketch, slots, ranks):
    panels = points.shape[2]
    width = sketch.shape[5]
    groups = sketch.shape[2]
    count = sketch.shape[3]
    helpers = lax.axis_size("help")
    others = helpers - 1
    chips = groups // 2
    chunk = panels // 4 if groups <= 8 else panels // 8
    chunks = panels // chunk
    col = lax.axis_index("help")

    scale = decay_rate * log2_e
    spot = (points[0, 0:3] - centre) * scale
    norm = jnp.sum(spot * spot, axis=0, keepdims=True)
    spots = jnp.concatenate([spot, norm], axis=0)
    blank = jnp.zeros((3, panels), jnp.float32)
    right = jnp.concatenate(
        [-2.0 * spot, jnp.ones((1, panels), jnp.float32), norm + soften * scale * scale, blank], axis=0
    )
    one, two, three = cut(right)
    feats = jnp.concatenate([one, two, one, two, three, one], axis=0).astype(jnp.bfloat16)
    logw = jnp.log2(points[0, 3:4]) + jnp.log2(jnp.float32(scale / four_pi))
    step = jnp.where(slots[0, 0] >= 0, (slots[0, 0] - col - 1) % helpers, -1)
    hot = (step[:, :, None] == jnp.arange(others, dtype=jnp.int32)).astype(jnp.float32)
    span = max(width, chunk)
    hot = jnp.broadcast_to(
        hot.reshape(chips, 2, count * others, 1, 1), (chips, 2, count * others, 1, span)
    )
    sizes = (chips, helpers, count, chunk, chunks, width)
    bf16, f32 = jnp.bfloat16, jnp.float32
    vmem = pl.BlockSpec(memory_space=pltpu.VMEM)
    dma = pltpu.SemaphoreType.DMA
    sums = pl.pallas_call(
        functools.partial(kernel, sizes),
        out_shape=jax.ShapeDtypeStruct((panels, width), f32),
        in_specs=[pl.BlockSpec(memory_space=pl.ANY), vmem, vmem, vmem, vmem],
        out_specs=vmem,
        scratch_shapes=[
            pltpu.VMEM((chips, count, panels, width), bf16),
            pltpu.VMEM((chips, count, panels, width), bf16),
            pltpu.VMEM((chips * helpers, 4, panels), f32),
            pltpu.VMEM((48, panels), bf16),
            pltpu.VMEM((1, panels), f32),
            pltpu.VMEM((chips, count * others, 1, span), f32),
            pltpu.VMEM((2 * count, 8, chunk), f32),
            pltpu.VMEM((others, chunk, width), f32),
            pltpu.VMEM((2, chips - 1, others, chunk, width), bf16),
            pltpu.VMEM((chunks, chips - 1, others, chunk, width), bf16),
            pltpu.VMEM((2, others, chunk, width), f32),
            pltpu.VMEM((chunks, others, chunk, width), bf16),
            pltpu.VMEM((chunks, others, chunk, width), bf16),
            dma((chips + 1,)),
            dma((chips,)),
            dma((chips,)),
            dma((chips * helpers,)),
            dma((chips * helpers,)),
            dma((3,)),
            dma((3,)),
            dma((2, chips - 1)),
            dma((chunks, chips - 1)),
            dma((chunks, others)),
            dma((chunks, others)),
        ],
        compiler_params=pltpu.CompilerParams(
            collective_id=0, has_side_effects=True, vmem_limit_bytes=60 * 1024 * 1024
        ),
    )(
        sketch.reshape(chips, 2, count, panels, width), spots, feats, logw, hot,
    )
    keep = jnp.arange(width, dtype=jnp.int32)[None, :] < ranks[0]
    kept = jnp.where(keep, sums, jnp.zeros_like(sums))[None]
    gram = jnp.einsum("usv,usw->uvw", kept, kept, precision=lax.Precision.HIGHEST)
    return kept, gram


def solution(mesh):
    in_specs = (
        P(("row", "help"), None, None),
        P("row", "help", None, None, None, None),
        P("row", "help", None, None),
        P(("row", "help")),
    )
    out_specs = (P(("row", "help"), None, None), P(("row", "help"), None, None))
    return jax.shard_map(
        per_device, mesh=mesh, in_specs=in_specs, out_specs=out_specs, check_vma=False
    )
```

time: 323 us -> 112 us (0.35)
  waiting for transfers between devices: 128 us -> 0 us
  blocking collectives: 107 us -> 0 us
  Pallas kernels: 0 us -> 96.5 us
  matrix products: 46.1 us -> 4.07 us
  local copies, waits for them, and re-layouts: 17.2 us -> 1.86 us
  between operations: 15.4 us -> 1.32 us
  starting transfers between devices: 5.14 us -> 0 us
    reduce_scatter x1 -> x0, waiting for transfers between devices: 128 us -> none  [per_device(): mine = lax.psum_scatter(sums, 'help', scatter_dimension=0, tiled=True)]
    all_gather x2 -> x0, blocking collectives: 97.3 us -> none  [the longest x1 84 us: per_device(): source_points = lax.all_gather(points, 'row', axis=0, tiled=True)]
    pallas_call x0 -> x1, Pallas kernels: none -> 96.5 us  [per_device(): pl.pallas_call(functools.partial(kernel, sizes), out_shape=jax.ShapeDtype...]
    dot_general x3 -> x1, matrix products: 46.1 us -> 4.07 us  [per_device(): jnp.einsum('usv,usw->uvw', kept, kept, precision=lax.Precision.HIGHEST)]
    all_to_all x1 -> x0, blocking collectives: 9.62 us -> none  [per_device(): lax.all_to_all(slots, 'row', split_axis=2, concat_axis=0, tiled=True)]
    gather x5 -> x0, local copies, waits for them, and re-layouts: 8.14 us -> none  [the longest x1 6.15 us: step(): products = multiply(tiles, arrived[indices])]
    all_to_all x1 -> x0, starting transfers between devices: 5.1 us -> none  [per_device(): lax.all_to_all(sketch, 'row', split_axis=2, concat_axis=0, tiled=True)]
    while x7 -> x0, local copies, waits for them, and re-layouts: 4.98 us -> none  [the longest x1 4.92 us: per_device(): sums = lax.fori_loop(0, turns, step, empty)]
  transfers between devices with their start and end apart: 2 -> 0, of which waited for: 1 -> 0; matrix products, arithmetic and copies ran while one was open for 1% -> 0% of each run, Pallas kernels for 0% -> 0%
where the time goes in v1:
time: 112 us; the launch traced here: 111 us
  Pallas kernels  96.5 us (86%)
  other arithmetic  6.83 us (6%)
  matrix products  4.07 us (4%)
  local copies, waits for them, and re-layouts  1.86 us (2%)
  between operations  1.32 us (1%)
    pallas_call x1, Pallas kernels, per_device(): pl.pallas_call(functools.partial(kernel, sizes), out_shape=jax.ShapeDtype...  96.5 us
    dot_general x1, matrix products, per_device(): jnp.einsum('usv,usw->uvw', kept, kept, precision=lax.Precision.HIGHEST)  4.07 us
    broadcast_in_dim x1, other arithmetic, per_device(): kept = jnp.where(keep, sums, jnp.zeros_like(sums))[None]  2.26 us

profile of v1, /device:TPU:0, one launch (start us, length us, event | category | flops | bytes accessed | tf_op | source)
XLA Modules:
  0.0 110.5 jit_solution(1588031272378298767)
XLA Ops:
  1.3 0.1 pad.1.clone
  1.4 0.7 bitcast_select_fusion
  2.1 0.1 pad.3.clone
  2.1 0.1 eq.28
  2.2 0.1 copy.7
  2.3 0.1 eq.25
  2.4 0.1 eq.26
  2.5 1.3 %add_bitcast_fusion.logw_ref = f32[1,1024]{1,0:T(1,128)} fusion(f32[1,4,1024]{2,1,0:T(4,128)} %param.4), kind=kLoop, calls=%fused_computation.24 | loop fusion | flops 2048 | bytes 8192 | tf_op jit(solution)/shard_map/add | solution.py:302
  3.8 0.7 multiply_reduce_fusion
  4.6 0.7 multiply_bitcast_fusion
  5.3 0.6 pad_maximum_fusion.spots_ref
  5.9 0.7 broadcast_in_dim.37.hot_ref
  6.6 0.1 constant_dynamic-update-slice_fusion.4
  6.7 0.1 constant_dynamic-update-slice_fusion.3
  6.8 0.1 constant_dynamic-update-slice_fusion.2
  6.9 0.1 constant_dynamic-update-slice_fusion.1
  6.9 0.1 fusion.5
  7.0 0.1 constant_dynamic-update-slice_fusion.feats_ref
  7.1 0.0 copy-start
  7.1 0.6 copy-done
  7.7 96.5 %shard_map.59 = f32[1024,256]{1,0:T(8,128)} custom-call(bf16[4,2,2,1024,256]{4,3,2,1,0:T(8,128)(2,1)} %bitcast.21, f32[4,1024]{1,0:T(4,128)} %pad_maximum_fusion.spots_ref, bf16[48,1024]{1,0:T(8,128)(2,1)} %copy-done, f32[1,1024]{1,0:T(1,128)} %add_bitcast_fusion.logw_ref, f32[4,2,6,1,256]{4,3,2,1,0:T(1,128)} %broadcast_in_dim.37.hot_ref), custom_call_target="tpu_custom_call" | custom-call | tf_op jit(solution)/shard_map/pallas_call | solution.py:313
  104.2 4.1 %convolution_bitcast_fusion = f32[1,256,256]{2,1,0:T(8,128)} fusion(f32[1024,256]{1,0:T(8,128)} %shard_map.59, pred[256]{0:T(512)(128)(4,1)S(1)} %iota_compare_fusion), kind=kOutput, calls=%fused_computation | convolution fusion | flops 805568512 | bytes 1310976 | tf_op jit(solution)/shard_map/usv,usw->uvw/dot_general | solution.py:352
  108.3 2.3 %select_bitcast_fusion = f32[1,1024,256]{2,1,0:T(8,128)} fusion(f32[1024,256]{1,0:T(8,128)} %shard_map.59, pred[256]{0:T(512)(128)(4,1)S(1)} %iota_compare_fusion), kind=kLoop, calls=%fused_computation.2 | loop fusion | flops 262144 | bytes 2097408 | tf_op jit(solution)/shard_map/broadcast_in_dim | solution.py:351
  (5 shorter events, 0.0 us)
Async XLA Ops:
  7.1 0.6 copy-start

commit v2 on v1

v2 whole, which is shorter than its diff:
```python
import functools

import jax
import jax.numpy as jnp
from jax import lax
from jax.experimental import pallas as pl
from jax.experimental.pallas import tpu as pltpu
from jax.sharding import PartitionSpec as P

decay_rate = 0.3
four_pi = 12.566370614359172
soften = 0.0025
log2_e = 1.4426950408889634
centre = 0.4
MESH = pl.DeviceIdType.MESH


def cut(value):
    first = lax.reduce_precision(value, 8, 7)
    rest = value - first
    second = lax.reduce_precision(rest, 8, 7)
    third = lax.reduce_precision(rest - second, 8, 7)
    return first, second, third


def kernel(
    sizes,
    sketch_ref, spots_ref, feats_ref, logw_ref, hot_ref, keep_ref,
    sums_ref, gram_ref,
    sk_own, sk_got, spots, feats_got, logw_got, hot_got,
    lhs, acc, far_send, far_recv, near_send, near_recv, z_send, z_recv,
    own_sem, sk_send_sem, sk_recv_sem, spot_send_sem, spot_recv_sem, side_send_sem, side_recv_sem,
    far_send_sem, far_recv_sem, near_send_sem, near_recv_sem, z_send_sem, z_recv_sem,
):
    chips, helpers, slots, chunk, chunks, width = sizes
    lines = chips // 2
    half = chunk // 2
    others = helpers - 1
    row = lax.axis_index("row")
    col = lax.axis_index("help")
    chip, core = row // 2, row % 2
    line, side = chip // 2, chip % 2
    sibling = chip * 2 + 1 - core
    peers = chips * helpers

    def chip_at(offset):
        return lax.rem(line + offset // 2, lines) * 2 + lax.rem(side + offset % 2, 2)

    def place(step):
        return (lax.rem(chip + step // helpers, chips), lax.rem(col + step % helpers, helpers))

    def back(step):
        return (
            lax.rem(chip + chips - step // helpers, chips),
            lax.rem(col + helpers - step % helpers, helpers),
        )

    barrier = pltpu.get_barrier_semaphore()

    @pl.loop(1, peers)
    def _(step):
        to_chip, to_col = place(step)
        pl.semaphore_signal(barrier, inc=1, device_id=(to_chip * 2 + core, to_col), device_id_type=MESH)

    pl.semaphore_signal(barrier, inc=1, device_id=(sibling, col), device_id_type=MESH)
    pl.semaphore_wait(barrier, peers)

    def remote(source, target, send_sem, recv_sem, to_row, to_col):
        return pltpu.make_async_remote_copy(
            src_ref=source,
            dst_ref=target,
            send_sem=send_sem,
            recv_sem=recv_sem,
            device_id=(to_row, to_col),
            device_id_type=MESH,
        )

    def spot_copy(step):
        to_chip, to_col = place(step)
        return remote(
            spots_ref, spots.at[chip * helpers + col],
            spot_send_sem.at[step], spot_recv_sem.at[step], to_chip * 2 + core, to_col,
        )

    def spot_arrival(step):
        from_chip, from_col = back(step)
        return remote(
            spots_ref, spots.at[from_chip * helpers + from_col],
            spot_send_sem.at[step], spot_recv_sem.at[step], from_chip * 2 + core, from_col,
        )

    def to_sibling(source, target, index):
        return remote(source, target, side_send_sem.at[index], side_recv_sem.at[index], sibling, col)

    sides = (
        to_sibling(feats_ref, feats_got, 0),
        to_sibling(logw_ref, logw_got, 1),
        to_sibling(hot_ref.at[:, 1 - core], hot_got, 2),
    )

    def sketch_copy(offset):
        group = chip_at(offset)
        return remote(
            sketch_ref.at[group, 1 - core], sk_got.at[group],
            sk_send_sem.at[offset], sk_recv_sem.at[offset], sibling, col,
        )

    def own_copy(offset):
        group = chip_at(offset)
        return pltpu.make_async_copy(sketch_ref.at[group, core], sk_own.at[group], own_sem.at[offset])

    own_spot = pltpu.make_async_copy(spots_ref, spots.at[chip * helpers + col], own_sem.at[chips])
    own_spot.start()

    @pl.loop(1, peers)
    def _(step):
        spot_copy(step).start()

    for each in sides:
        each.start()

    @pl.loop(0, chips)
    def _(turn):
        offset = chips - 1 - turn
        sketch_copy(offset).start()
        own_copy(offset).start()

    lhs[...] = jnp.where(
        lax.broadcasted_iota(jnp.int32, lhs.shape, 1) == 4, jnp.float32(1), jnp.float32(0)
    )
    gram_ref[...] = jnp.zeros_like(gram_ref)
    own_spot.wait()
    for each in sides:
        each.wait()

    @pl.loop(1, peers)
    def _(step):
        spot_copy(step).wait_send()
        spot_arrival(step).wait_recv()

    def rows_of(index):
        return pl.ds(pl.multiple_of(index * chunk, chunk), chunk)

    def block(index, group, sketches, feats, logw, hot_rows, slot, unit):
        spot = jnp.zeros((4, chunk), jnp.float32)
        hots = []
        for step in range(others):
            hot = hot_rows(slot * others + step)
            hots.append(hot)
            target = group * helpers + lax.rem(col + 1 + step, helpers)
            spot = spot + hot[:, :chunk] * spots[target, :, rows_of(index)]
        lhs[unit, 0:4, :] = spot
        full = lhs[unit]
        one = full.astype(jnp.bfloat16).astype(jnp.float32)
        rest = full - one
        two = rest.astype(jnp.bfloat16).astype(jnp.float32)
        three = rest - two
        stack = jnp.concatenate([one, one, two, two, one, three], axis=0)
        left = stack.T.astype(jnp.bfloat16)
        square = jnp.dot(left, feats, preferred_element_type=jnp.float32)
        inverse = lax.rsqrt(square)
        tile = (jnp.exp2(logw - square * inverse) * inverse).astype(jnp.bfloat16)
        product = jnp.dot(tile, sketches, preferred_element_type=jnp.float32)
        return [hot[:, :width] * product for hot in hots]

    def compute(index, offset):
        group = chip_at(offset)
        totals = [None] * others
        for slot in range(slots):
            mine = block(
                index, group, sk_own[group, slot], feats_ref[...], logw_ref[...],
                lambda at: hot_ref[group, core, at], slot, slot,
            )
            theirs = block(
                index, group, sk_got[group, slot], feats_got[...], logw_got[...],
                lambda at: hot_got[group, at], slot, slots + slot,
            )
            for step in range(others):
                part = mine[step] + theirs[step]
                totals[step] = part if totals[step] is None else totals[step] + part
        return totals

    def far_copy(index, way, hop):
        to_chip = chip_at(1) if way == 0 else chip_at(2 * (hop + 1))
        return remote(
            far_send.at[index % 2, way, hop], far_recv.at[index, way, hop],
            far_send_sem.at[index % 2, way, hop], far_recv_sem.at[index, way, hop],
            to_chip * 2 + core, col,
        )

    def near_offset(at):
        return jnp.where(at == lines - 1, 1, 2 * (at + 1))

    def near_copy(index, at):
        return remote(
            near_send.at[index % 2, at], near_recv.at[index, at],
            near_send_sem.at[index % 2, at], near_recv_sem.at[index, at],
            chip_at(near_offset(at)) * 2 + core, col,
        )

    def z_copy(index, step):
        return remote(
            z_send.at[index % 2, step], z_recv.at[index, step],
            z_send_sem.at[index % 2, step], z_recv_sem.at[index, step],
            row, lax.rem(col + 1 + step, helpers),
        )

    def send_far(index):
        @pl.loop(0, lines - 1)
        def _(hop):
            offset = 2 * (hop + 1) + 1

            @pl.when(index == 0)
            def _():
                own_copy(offset).wait()
                sketch_copy(offset).wait()

            @pl.when(index >= 2)
            def _():
                for way in range(2):
                    far_copy(index, way, hop).wait_send()

            totals = compute(index, offset)
            for way in range(2):
                for step in range(others):
                    far_send[index % 2, way, hop, step] = totals[step][
                        way * half : (way + 1) * half
                    ].astype(jnp.bfloat16)
                far_copy(index, way, hop).start()

    def send_near(index):
        @pl.loop(0, lines + 1)
        def _(at):
            offset = jnp.where(at == lines, 0, near_offset(at))

            @pl.when(index == 0)
            def _():
                own_copy(offset).wait()
                sketch_copy(offset).wait()

            totals = compute(index, offset)
            for step in range(others):
                acc[at + jnp.where(at == lines, index % 2, 0), step] = totals[step]

        @pl.when(index >= 2)
        def _():
            @pl.loop(0, lines)
            def _(at):
                near_copy(index, at).wait_send()

        @pl.loop(0, lines - 1)
        def _(hop):
            far_copy(index, 0, hop).wait_recv()
            far_copy(index, 1, hop).wait_recv()
            for step in range(others):
                near_send[index % 2, hop, step, :half] = (
                    acc[hop, step, :half] + far_recv[index, 0, hop, step].astype(jnp.float32)
                ).astype(jnp.bfloat16)
                near_send[index % 2, hop, step, half:] = acc[hop, step, half:].astype(jnp.bfloat16)
                acc[lines - 1, step, half:] += far_recv[index, 1, hop, step].astype(jnp.float32)
            near_copy(index, hop).start()

        for step in range(others):
            near_send[index % 2, lines - 1, step] = acc[lines - 1, step].astype(jnp.bfloat16)
        near_copy(index, lines - 1).start()

    def gather(index):
        @pl.loop(0, lines)
        def _(at):
            near_copy(index, at).wait_recv()

        for step in range(others):
            total = acc[lines + index % 2, step]
            for at in range(lines):
                total = total + near_recv[index, at, step].astype(jnp.float32)

            @pl.when(index >= 2)
            def _():
                z_copy(index, step).wait_send()

            z_send[index % 2, step] = total.astype(jnp.bfloat16)
            z_copy(index, step).start()

    def finish(index):
        total = None
        for step in range(others):
            z_copy(index, step).wait_recv()
            part = z_recv[index, step].astype(jnp.float32)
            total = part if total is None else total + part
        total = jnp.where(keep_ref[...] > 0, total, jnp.zeros_like(total))
        sums_ref[rows_of(index), :] = total
        gram_ref[...] += lax.dot_general(
            total, total, (((0,), (0,)), ((), ())),
            precision=lax.Precision.HIGHEST, preferred_element_type=jnp.float32,
        )

    @pl.loop(0, chunks + 3)
    def _(turn):
        @pl.when(turn < chunks)
        def _():
            send_far(turn)

        @pl.when((turn >= 1) & (turn < chunks + 1))
        def _():
            send_near(turn - 1)

        @pl.when((turn >= 2) & (turn < chunks + 2))
        def _():
            gather(turn - 2)

        @pl.when(turn >= 3)
        def _():
            finish(turn - 3)

    for index in (chunks - 2, chunks - 1):
        @pl.loop(0, lines - 1)
        def _(hop):
            for way in range(2):
                far_copy(index, way, hop).wait_send()

        @pl.loop(0, lines)
        def _(at):
            near_copy(index, at).wait_send()

        for step in range(others):
            z_copy(index, step).wait_send()


def per_device(points, sketch, slots, ranks):
    panels = points.shape[2]
    width = sketch.shape[5]
    groups = sketch.shape[2]
    count = sketch.shape[3]
    helpers = lax.axis_size("help")
    others = helpers - 1
    chips = groups // 2
    chunk = panels // 8
    lines = chips // 2
    half = chunk // 2
    chunks = panels // chunk
    col = lax.axis_index("help")

    scale = decay_rate * log2_e
    spot = (points[0, 0:3] - centre) * scale
    norm = jnp.sum(spot * spot, axis=0, keepdims=True)
    spots = jnp.concatenate([spot, norm], axis=0)
    blank = jnp.zeros((3, panels), jnp.float32)
    right = jnp.concatenate(
        [-2.0 * spot, jnp.ones((1, panels), jnp.float32), norm + soften * scale * scale, blank], axis=0
    )
    one, two, three = cut(right)
    feats = jnp.concatenate([one, two, one, two, three, one], axis=0).astype(jnp.bfloat16)
    logw = jnp.log2(points[0, 3:4]) + jnp.log2(jnp.float32(scale / four_pi))
    step = jnp.where(slots[0, 0] >= 0, (slots[0, 0] - col - 1) % helpers, -1)
    hot = (step[:, :, None] == jnp.arange(others, dtype=jnp.int32)).astype(jnp.float32)
    span = max(width, chunk)
    hot = jnp.broadcast_to(
        hot.reshape(chips, 2, count * others, 1, 1), (chips, 2, count * others, 1, span)
    )
    sizes = (chips, helpers, count, chunk, chunks, width)
    bf16, f32 = jnp.bfloat16, jnp.float32
    vmem = pl.BlockSpec(memory_space=pltpu.VMEM)
    dma = pltpu.SemaphoreType.DMA
    keep = (jnp.arange(width, dtype=jnp.int32)[None, :] < ranks[0]).astype(f32)
    sums, gram = pl.pallas_call(
        functools.partial(kernel, sizes),
        out_shape=(
            jax.ShapeDtypeStruct((panels, width), f32),
            jax.ShapeDtypeStruct((width, width), f32),
        ),
        in_specs=[pl.BlockSpec(memory_space=pl.ANY), vmem, vmem, vmem, vmem, vmem],
        out_specs=(vmem, vmem),
        scratch_shapes=[
            pltpu.VMEM((chips, count, panels, width), bf16),
            pltpu.VMEM((chips, count, panels, width), bf16),
            pltpu.VMEM((chips * helpers, 4, panels), f32),
            pltpu.VMEM((48, panels), bf16),
            pltpu.VMEM((1, panels), f32),
            pltpu.VMEM((chips, count * others, 1, span), f32),
            pltpu.VMEM((2 * count, 8, chunk), f32),
            pltpu.VMEM((lines + 2, others, chunk, width), f32),
            pltpu.VMEM((2, 2, lines - 1, others, half, width), bf16),
            pltpu.VMEM((chunks, 2, lines - 1, others, half, width), bf16),
            pltpu.VMEM((2, lines, others, chunk, width), bf16),
            pltpu.VMEM((chunks, lines, others, chunk, width), bf16),
            pltpu.VMEM((2, others, chunk, width), bf16),
            pltpu.VMEM((chunks, others, chunk, width), bf16),
            dma((chips + 1,)),
            dma((chips,)),
            dma((chips,)),
            dma((chips * helpers,)),
            dma((chips * helpers,)),
            dma((3,)),
            dma((3,)),
            dma((2, 2, lines - 1)),
            dma((chunks, 2, lines - 1)),
            dma((2, lines)),
            dma((chunks, lines)),
            dma((2, others)),
            dma((chunks, others)),
        ],
        compiler_params=pltpu.CompilerParams(
            collective_id=0, has_side_effects=True, vmem_limit_bytes=62 * 1024 * 1024
        ),
    )(
        sketch.reshape(chips, 2, count, panels, width), spots, feats, logw, hot, keep,
    )
    return sums[None], gram[None]


def solution(mesh):
    in_specs = (
        P(("row", "help"), None, None),
        P("row", "help", None, None, None, None),
        P("row", "help", None, None),
        P(("row", "help")),
    )
    out_specs = (P(("row", "help"), None, None), P(("row", "help"), None, None))
    return jax.shard_map(
        per_device, mesh=mesh, in_specs=in_specs, out_specs=out_specs, check_vma=False
    )
```

time: 112 us -> 90.2 us (0.81)
  Pallas kernels: 96.5 us -> 77.5 us
  matrix products: 4.07 us -> 0 us
  local copies, waits for them, and re-layouts: 1.86 us -> 5.79 us
  other arithmetic: 6.83 us -> 5.13 us
    pallas_call x1, Pallas kernels: 96.5 us -> 77.5 us  [per_device(): pl.pallas_call(functools.partial(kernel, sizes), out_shape=(jax.ShapeDtyp...]
    dot_general x1 -> x0, matrix products: 4.07 us -> none  [per_device(): jnp.einsum('usv,usw->uvw', kept, kept, precision=lax.Precision.HIGHEST)]
    unnamed x2 -> x4, local copies, waits for them, and re-layouts: 0.64 us -> 4.57 us
    broadcast_in_dim x1 -> x0, other arithmetic: 2.26 us -> none  [per_device(): kept = jnp.where(keep, sums, jnp.zeros_like(sums))[None]]
where the time goes in v2:
time: 90.2 us; the launch traced here: 89.7 us
  Pallas kernels  77.5 us (86%)
  local copies, waits for them, and re-layouts  5.79 us (6%)
  other arithmetic  5.13 us (6%)
  between operations  1.32 us (1%)
    pallas_call x1, Pallas kernels, per_device(): pl.pallas_call(functools.partial(kernel, sizes), out_shape=(jax.ShapeDtyp...  77.5 us
    unnamed x4, local copies, waits for them, and re-layouts  4.57 us

profile of v2, /device:TPU:0, one launch (start us, length us, event | category | flops | bytes accessed | tf_op | source)
XLA Modules:
  0.0 89.7 jit_solution(12980256526061810626)
XLA Ops:
  1.3 0.1 pad.1.clone
  1.4 0.7 bitcast_select_fusion
  2.0 0.6 compare_convert_fusion.1.keep_ref
  2.6 0.1 pad.3.clone
  2.7 0.1 eq.28
  2.8 0.1 copy.7
  2.9 0.1 eq.25
  3.0 0.1 eq.26
  3.0 1.3 %add_bitcast_fusion.logw_ref = f32[1,1024]{1,0:T(1,128)} fusion(f32[1,4,1024]{2,1,0:T(4,128)} %param.4), kind=kLoop, calls=%fused_computation.19 | loop fusion | flops 2048 | bytes 8192 | tf_op jit(solution)/shard_map/add | solution.py:353
  4.4 0.7 multiply_reduce_fusion
  5.1 0.7 multiply_bitcast_fusion
  5.9 0.6 pad_maximum_fusion.spots_ref
  6.5 0.7 broadcast_in_dim.28.hot_ref
  7.2 0.1 constant_dynamic-update-slice_fusion.4
  7.3 0.1 constant_dynamic-update-slice_fusion.3
  7.4 0.1 constant_dynamic-update-slice_fusion.2
  7.4 0.1 constant_dynamic-update-slice_fusion.1
  7.5 0.1 fusion.2
  7.6 0.1 constant_dynamic-update-slice_fusion.feats_ref
  7.7 0.0 copy-start
  7.7 0.6 copy-done
  8.3 77.5 %shard_map.59 = (f32[1024,256]{1,0:T(8,128)}, f32[256,256]{1,0:T(8,128)}) custom-call(bf16[4,2,2,1024,256]{4,3,2,1,0:T(8,128)(2,1)} %bitcast.19, f32[4,1024]{1,0:T(4,128)} %pad_maximum_fusion.spots_ref, bf16[48,1024]{1,0:T(8,128)(2,1)} %copy-done, f32[1,1024]{1,0:T(1,128)} %add_bitcast_fusion.logw_ref, f32[4,2,6,1,256]{4,3,2,1,0:T(1,128)} %broadcast_in_dim.28.hot_ref, ...), custom_call_target="tpu_custom_call" | custom-call | tf_op jit(solution)/shard_map/pallas_call | solution.py:365
  85.8 2.3 %copy.16 = f32[1,1024,256]{2,1,0:T(8,128)} copy(f32[1,1024,256]{2,1,0:T(8,128)} %bitcast.20) | data formatting | bytes 2097152
  88.0 1.7 %copy.17 = f32[1,256,256]{2,1,0:T(8,128)} copy(f32[1,256,256]{2,1,0:T(8,128)} %bitcast.21) | data formatting | bytes 524288
  (4 shorter events, 0.0 us)
Async XLA Ops:
  7.7 0.6 copy-start

commit v3 on v2

--- a/solution.py
+++ b/solution.py
@@ -16,18 +16,17 @@
 
 
 def cut(value):
-    first = lax.reduce_precision(value, 8, 7)
+    first = value.astype(jnp.bfloat16).astype(jnp.float32)
     rest = value - first
-    second = lax.reduce_precision(rest, 8, 7)
-    third = lax.reduce_precision(rest - second, 8, 7)
-    return first, second, third
+    second = rest.astype(jnp.bfloat16).astype(jnp.float32)
+    return first, second, rest - second
 
 
 def kernel(
     sizes,
-    sketch_ref, spots_ref, feats_ref, logw_ref, hot_ref, keep_ref,
+    sketch_ref, points_ref, hot_ref, keep_ref,
     sums_ref, gram_ref,
-    sk_own, sk_got, spots, feats_got, logw_got, hot_got,
+    spots_ref, right, feats_ref, logw_ref, sk_own, sk_got, spots, feats_got, logw_got, hot_got,
     lhs, acc, far_send, far_recv, near_send, near_recv, z_send, z_recv,
     own_sem, sk_send_sem, sk_recv_sem, spot_send_sem, spot_recv_sem, side_send_sem, side_recv_sem,
     far_send_sem, far_recv_sem, near_send_sem, near_recv_sem, z_send_sem, z_recv_sem,
@@ -63,6 +62,20 @@
         pl.semaphore_signal(barrier, inc=1, device_id=(to_chip * 2 + core, to_col), device_id_type=MESH)
 
     pl.semaphore_signal(barrier, inc=1, device_id=(sibling, col), device_id_type=MESH)
+
+    scale = decay_rate * log2_e
+    spot = (points_ref[0:3, :] - centre) * scale
+    norm = jnp.sum(spot * spot, axis=0, keepdims=True)
+    spots_ref[0:3, :] = spot
+    spots_ref[3:4, :] = norm
+    right[...] = jnp.zeros_like(right)
+    right[0:3, :] = -2.0 * spot
+    right[3:4, :] = jnp.ones_like(norm)
+    right[4:5, :] = norm + soften * scale * scale
+    one, two, three = cut(right[...])
+    feats_ref[...] = jnp.concatenate([one, two, one, two, three, one], axis=0).astype(jnp.bfloat16)
+    logw_ref[...] = jnp.log(points_ref[3:4, :] * (scale / four_pi)) * log2_e
+
     pl.semaphore_wait(barrier, peers)
 
     def remote(source, target, send_sem, recv_sem, to_row, to_col):
@@ -340,17 +353,6 @@
     chunks = panels // chunk
     col = lax.axis_index("help")
 
-    scale = decay_rate * log2_e
-    spot = (points[0, 0:3] - centre) * scale
-    norm = jnp.sum(spot * spot, axis=0, keepdims=True)
-    spots = jnp.concatenate([spot, norm], axis=0)
-    blank = jnp.zeros((3, panels), jnp.float32)
-    right = jnp.concatenate(
-        [-2.0 * spot, jnp.ones((1, panels), jnp.float32), norm + soften * scale * scale, blank], axis=0
-    )
-    one, two, three = cut(right)
-    feats = jnp.concatenate([one, two, one, two, three, one], axis=0).astype(jnp.bfloat16)
-    logw = jnp.log2(points[0, 3:4]) + jnp.log2(jnp.float32(scale / four_pi))
     step = jnp.where(slots[0, 0] >= 0, (slots[0, 0] - col - 1) % helpers, -1)
     hot = (step[:, :, None] == jnp.arange(others, dtype=jnp.int32)).astype(jnp.float32)
     span = max(width, chunk)
@@ -368,9 +370,13 @@
             jax.ShapeDtypeStruct((panels, width), f32),
             jax.ShapeDtypeStruct((width, width), f32),
         ),
-        in_specs=[pl.BlockSpec(memory_space=pl.ANY), vmem, vmem, vmem, vmem, vmem],
+        in_specs=[pl.BlockSpec(memory_space=pl.ANY), vmem, vmem, vmem],
         out_specs=(vmem, vmem),
         scratch_shapes=[
+            pltpu.VMEM((4, panels), f32),
+            pltpu.VMEM((8, panels), f32),
+            pltpu.VMEM((48, panels), bf16),
+            pltpu.VMEM((1, panels), f32),
             pltpu.VMEM((chips, count, panels, width), bf16),
             pltpu.VMEM((chips, count, panels, width), bf16),
             pltpu.VMEM((chips * helpers, 4, panels), f32),
@@ -403,7 +409,7 @@
             collective_id=0, has_side_effects=True, vmem_limit_bytes=62 * 1024 * 1024
         ),
     )(
-        sketch.reshape(chips, 2, count, panels, width), spots, feats, logw, hot, keep,
+        sketch.reshape(chips, 2, count, panels, width), points[0], hot, keep,
     )
     return sums[None], gram[None]
 

time: 90.2 us -> 85.2 us (0.945)
  other arithmetic: 5.13 us -> 1.26 us
    add x2 -> x0, other arithmetic: 1.33 us -> none  [the longest x1 1.32 us: per_device(): logw = jnp.log2(points[0, 3:4]) + jnp.log2(jnp.float32(scale / four_pi))]
    unnamed x4 -> x2, local copies, waits for them, and re-layouts: 4.57 us -> 3.93 us
where the time goes in v3:
time: 85.2 us; the launch traced here: 84.9 us
  Pallas kernels  77.4 us (91%)
  local copies, waits for them, and re-layouts  5.01 us (6%)
  between operations  1.29 us (2%)
  other arithmetic  1.26 us (1%)
    pallas_call x1, Pallas kernels, per_device(): pl.pallas_call(functools.partial(kernel, sizes), out_shape=(jax.ShapeDtyp...  77.4 us
    unnamed x2, local copies, waits for them, and re-layouts  3.93 us

profile of v3, /device:TPU:0, one launch (start us, length us, event | category | flops | bytes accessed | tf_op | source)
XLA Modules:
  0.0 84.9 jit_solution(9070728223078422562)
XLA Ops:
  1.3 0.7 bitcast_select_fusion
  2.0 0.6 compare_convert_fusion.1.keep_ref
  2.5 0.1 eq.28
  2.6 0.1 copy.7
  2.7 0.1 eq.25
  2.8 0.1 eq.26
  2.9 0.7 broadcast_in_dim.8.hot_ref
  3.6 77.4 %shard_map.59 = (f32[1024,256]{1,0:T(8,128)}, f32[256,256]{1,0:T(8,128)}) custom-call(bf16[4,2,2,1024,256]{4,3,2,1,0:T(8,128)(2,1)} %bitcast.10, f32[4,1024]{1,0:T(4,128)} %bitcast.13, f32[4,2,6,1,256]{4,3,2,1,0:T(1,128)} %broadcast_in_dim.8.hot_ref, f32[1,256]{1,0:T(1,128)} %compare_convert_fusion.1.keep_ref), custom_call_target="tpu_custom_call" | custom-call | tf_op jit(solution)/shard_map/pallas_call | solution.py:367
  81.0 2.3 %copy.11 = f32[1,1024,256]{2,1,0:T(8,128)} copy(f32[1,1024,256]{2,1,0:T(8,128)} %bitcast.11) | data formatting | bytes 2097152
  83.3 1.7 %copy.12 = f32[1,256,256]{2,1,0:T(8,128)} copy(f32[1,256,256]{2,1,0:T(8,128)} %bitcast.12) | data formatting | bytes 524288
  (2 shorter events, 0.0 us)
